TPU v7x, 32 devices: a whole 2x2x4 slice. The times are simulated.
32 devices in a mesh: dp: 8 (over y, x, core), tensor: 4 (over z).
Axes of the slice: x: 2, y: 2, z: 4, core: 2. Of those that a mesh axis runs over, the one named last changes fastest.
Arguments:
- activations: bfloat16 [4096, 8192], P('dp'), may hold values from -6 to 6
- cotangent: bfloat16 [4096, 14336], P('dp', 'tensor'), may hold values from -40 to 40
- gate_weight: bfloat16 [8192, 14336], P('dp', 'tensor'), may hold values from -0.046875 to 0.046875
- basis: bfloat16 [8192, 256], replicated, may hold values from -13 to 13
- first_moment: float32 [256, 14336], P('dp', 'tensor'), may hold values from -0.0078125 to 0.0078125
- second_moment: float32 [256, 14336], P('dp', 'tensor'), may hold values from 5e-08 to 1e-06
Outputs:
- input_grad: bfloat16 [4096, 8192], P('dp', 'tensor')
- weight_step: bfloat16 [8192, 14336], P('dp', 'tensor')
- new_first: float32 [256, 14336], P('dp', 'tensor')
- new_second: float32 [256, 14336], P('dp', 'tensor')
All inputs are finite; a program needn't handle non-finite values.
Results may differ from a plain program's by a relative error of at most 0.017.
Values may be sent and summed in bfloat16 or wider, within the bound.
A program may use at most 192 MiB of HBM per device.

v0:
```python
import jax
import jax.numpy as jnp
from jax import lax
from jax.sharding import PartitionSpec as P

beta_one = 0.9
beta_two = 0.999
adam_epsilon = 1e-08
adam_count = 10.0
norm_epsilon = 1e-06


def on_device(activations, cotangent, gate_weight, basis, first_moment, second_moment):
    dp_index = lax.axis_index("dp")
    own_rows = gate_weight.shape[0]
    partial_value = lax.dot_general(
        cotangent,
        lax.all_gather(gate_weight, "dp", axis=0, tiled=True),
        (((1,), (1,)), ((), ())),
        preferred_element_type=jnp.float32,
    )
    summand = lax.optimization_barrier(partial_value.astype(jnp.bfloat16)).astype(jnp.float32)
    input_grad = lax.psum_scatter(
        summand.astype(jnp.bfloat16), "tensor", scatter_dimension=1, tiled=True
    )
    coords = jnp.dot(activations, basis, preferred_element_type=jnp.float32).astype(jnp.bfloat16)
    owned = lax.psum_scatter(
        lax.dot_general(
            coords, cotangent, (((0,), (0,)), ((), ())), preferred_element_type=jnp.float32
        ).astype(jnp.bfloat16),
        "dp",
        scatter_dimension=0,
        tiled=True,
    ).astype(jnp.float32)
    total = lax.psum(jnp.sum(owned * owned), ("dp", "tensor"))
    factor = 1.0 / jnp.sqrt(total + norm_epsilon)
    scaled = factor * owned
    new_first = beta_one * first_moment + (1.0 - beta_one) * scaled
    new_second = beta_two * second_moment + (1.0 - beta_two) * scaled * scaled
    first_hat = new_first / (1.0 - beta_one**adam_count)
    second_hat = new_second / (1.0 - beta_two**adam_count)
    direction = (first_hat / (jnp.sqrt(second_hat) + adam_epsilon)).astype(jnp.bfloat16)
    basis_rows = lax.dynamic_slice_in_dim(basis, dp_index * own_rows, own_rows, 0)
    expanded = jnp.dot(
        basis_rows,
        lax.all_gather(direction, "dp", axis=0, tiled=True),
        preferred_element_type=jnp.float32,
    )
    weight_step = expanded.astype(jnp.bfloat16)
    return (input_grad, weight_step, new_first, new_second)


def solution(mesh):
    in_specs = (
        P("dp", None),
        P("dp", "tensor"),
        P("dp", "tensor"),
        P(),
        P("dp", "tensor"),
        P("dp", "tensor"),
    )
    out_specs = (P("dp", "tensor"), P("dp", "tensor"), P("dp", "tensor"), P("dp", "tensor"))
    return jax.shard_map(
        on_device, mesh=mesh, in_specs=in_specs, out_specs=out_specs, check_vma=False
    )
```

profile of v0, /device:TPU:7, one launch (start us, length us, event | category | flops | bytes accessed | tf_op | source)
XLA Modules:
  0.0 522.2 jit_solution(15443660001835894714)
XLA Ops:
  7.2 0.0 reduce-scatter.5.cloned.1.call-start
  7.2 12.2 %convolution_convert_fusion.2 = bf16[256,3584]{1,0:T(8,128)(2,1)} fusion(bf16[512,3584]{1,0:T(8,128)(2,1)} %param.7, bf16[512,8192]{1,0:T(8,128)(2,1)} %param.6, bf16[8192,256]{1,0:T(8,128)(2,1)} %param.9), kind=kOutput, calls=%fused_computation.2 | convolution fusion | flops 3088056320 | bytes 18087936 | tf_op jit(solution)/shard_map/dot_general | solution.py:28
  19.4 0.0 reduce-scatter.5.cloned.1.call-update
  19.4 0.0 copy-start
  19.4 0.0 copy-start.1
  19.4 0.0 all-gather.3.cloned.1.call-start
  19.5 0.7 all-gather.3.cloned.1.call-update
  20.2 0.0 all-gather.5.cloned.1.call-start
  20.2 39.2 %reduce-scatter.5.cloned.1.call-done = bf16[32,3584]{1,0:T(8,128)(2,1)} async-done(((bf16[256,3584]{1,0:T(8,128)(2,1)}), bf16[32,3584]{1,0:T(8,128)(2,1)}) %reduce-scatter.5.cloned.1.call-update) | async-done | bytes 229392 | tf_op jit(solution)/shard_map/reduce_scatter | solution.py:27
  59.5 1.7 fusion.3
  61.2 40.0 %psum.7 = f32[]{:T(128)} all-reduce(f32[]{:T(128)} %fusion.3), channel_id=1, replica_groups=mesh['dp'=8,'tensor'=4] {'dp','tensor'}, use_global_device_ids=true, to_apply=%region_3.0 | all-reduce | flops 1 | bytes 8 | tf_op jit(solution)/shard_map/psum | solution.py:35
  101.8 0.0 copy-done
  101.8 0.0 copy-done.1
  101.8 2.1 divide_convert_fusion
  103.9 0.0 all-gather.5.cloned.1.call-update
  104.0 0.0 reduce-scatter.3.cloned.1.call-start
  104.0 225.9 %all-gather.3.cloned.1.call-done = bf16[8192,3584]{1,0:T(8,128)(2,1)} async-done(((bf16[1024,3584]{1,0:T(8,128)(2,1)}), bf16[8192,3584]{1,0:T(8,128)(2,1)}) %all-gather.3.cloned.1.call-update) | async-done | bytes 58720272 | tf_op jit(solution)/shard_map/all_gather | solution.py:18
  329.9 40.8 %convolution_convert_fusion = bf16[512,8192]{1,0:T(8,128)(2,1)} fusion(bf16[512,3584]{1,0:T(8,128)(2,1)} %param.7, bf16[8192,3584]{1,0:T(8,128)(2,1)} %all-gather.3.cloned.1.call-done), kind=kOutput, calls=%fused_computation | convolution fusion | flops 30068965376 | bytes 70778880 | tf_op jit(solution)/shard_map/dot_general | solution.py:16
  370.7 0.0 reduce-scatter.3.cloned.1.call-update
  370.7 0.0 all-gather.5.cloned.1.call-done
  370.8 6.8 %convolution_convert_fusion.1 = bf16[1024,3584]{1,0:T(8,128)(2,1)} fusion(bf16[256,3584]{1,0:T(8,128)(2,1)} %all-gather.5.cloned.1.call-done, bf16[8192,256]{1,0:T(8,128)(2,1)} %param.9, s32[]{:T(128)S(6)} %select_n.3), kind=kOutput, calls=%fused_computation.1 | convolution fusion | flops 1882718208 | bytes 9699332 | tf_op jit(solution)/shard_map/dot_general | solution.py:44
  377.6 138.1 %reduce-scatter.3.cloned.1.call-done = bf16[512,2048]{1,0:T(8,128)(2,1)} async-done(((bf16[512,8192]{1,0:T(8,128)(2,1)}), bf16[512,2048]{1,0:T(8,128)(2,1)}) %reduce-scatter.3.cloned.1.call-update) | async-done | bytes 2097168 | tf_op jit(solution)/shard_map/reduce_scatter | solution.py:23
Async XLA Ops:
  7.2 52.3 %reduce-scatter.5.cloned.1.call-start = ((), (), s32[]{:S(2)}) async-start(), calls=%async_computation.4 | async-start | bytes 2064384 | tf_op jit(solution)/shard_map/reduce_scatter | solution.py:27
  19.4 82.4 %copy-start = (f32[32,3584]{1,0:T(8,128)S(1)}, f32[32,3584]{1,0:T(8,128)}, u32[]{:S(2)}) copy-start(f32[32,3584]{1,0:T(8,128)} %param.10) | copy-start | bytes 1376260
  19.4 82.4 %copy-start.1 = (f32[32,3584]{1,0:T(8,128)S(1)}, f32[32,3584]{1,0:T(8,128)}, u32[]{:S(2)}) copy-start(f32[32,3584]{1,0:T(8,128)} %param.11) | copy-start | bytes 1376260
  19.4 310.5 %all-gather.3.cloned.1.call-start = ((), (), s32[]{:S(2)}) async-start(), calls=%async_computation.2 | async-start | bytes 66060288 | tf_op jit(solution)/shard_map/all_gather | solution.py:18
  20.2 350.6 %all-gather.5.cloned.1.call-start = ((), (), s32[]{:S(2)}) async-start(), calls=%async_computation.5 | async-start | bytes 2064384 | tf_op jit(solution)/shard_map/all_gather | solution.py:46
  104.0 411.7 %reduce-scatter.3.cloned.1.call-start = ((), (), s32[]{:S(2)}) async-start(), calls=%async_computation.3 | async-start | bytes 10485760 | tf_op jit(solution)/shard_map/reduce_scatter | solution.py:23
Sparse Core Ops, SparseCore 0:
  19.5 39.9 reduce-scatter.4
  61.4 268.4 all-gather.2
  332.4 26.7 all-gather.4
  370.9 144.7 reduce-scatter.2
where the time goes:
time: 524 us; the launch traced here: 522 us
  waiting for transfers between devices  404 us (77%)
  matrix products  59.8 us (11%)
  blocking collectives  40 us (8%)
  between operations  14.5 us (3%)
    all_gather x1, waiting for transfers between devices, on_device(): lax.all_gather(gate_weight, 'dp', axis=0, tiled=True)  226 us
    reduce_scatter x1, waiting for transfers between devices, on_device(): lax.psum_scatter(summand.astype(jnp.bfloat16), 'tensor', scatter_dimensio...  138 us
    dot_general x1, matrix products, on_device(): lax.dot_general(cotangent, lax.all_gather(gate_weight, 'dp', axis=0, tile...  40.8 us
    psum x1, blocking collectives, on_device(): total = lax.psum(jnp.sum(owned * owned), ('dp', 'tensor'))  40 us
    reduce_scatter x1, waiting for transfers between devices, on_device(): lax.psum_scatter(lax.dot_general(coords, cotangent, (((0,), (0,)), ((), (...  39.2 us
    dot_general x1, matrix products, on_device(): lax.dot_general(coords, cotangent, (((0,), (0,)), ((), ())), preferred_el...  12.2 us
  transfers between devices with their start and end apart: 4, of which 3 were waited for; matrix products, arithmetic and copies ran while one was open for 10% of the time, Pallas kernels for 0%

commit v1 on v0

v1 whole, which is shorter than its diff:
```python
import functools

import jax
import jax.numpy as jnp
from jax import lax
from jax.sharding import PartitionSpec as P

beta_one = 0.9
beta_two = 0.999
adam_epsilon = 1e-08
adam_count = 10.0
norm_epsilon = 1e-06

x_pieces = 4
early_pieces = 2


def product(left, right):
    return lax.dot_general(
        left, right, (((1,), (1,)), ((), ())), preferred_element_type=jnp.float32
    ).astype(jnp.bfloat16)


def add(left, right):
    return (left.astype(jnp.float32) + right.astype(jnp.float32)).astype(left.dtype)


def on_device(dp_n, z_n, activations, cotangent, gate_weight, basis, first_moment, second_moment):
    high_n = dp_n // 4
    me = lax.axis_index("dp")
    z = lax.axis_index("tensor")
    own_rows = gate_weight.shape[0]

    def swap(value, mask):
        return lax.ppermute(value, "dp", [(i, i ^ mask) for i in range(dp_n)])

    def reduce_block(value, offset):
        for step in range(1, z_n):
            pairs = []
            for i in range(dp_n):
                owner = (i // 2) ^ offset
                if step - 1 < owner:
                    pairs.append((i * z_n + step - 1, i * z_n + step))
                if z_n - step > owner:
                    pairs.append((i * z_n + z_n - step, i * z_n + z_n - step - 1))
            value = add(value, lax.ppermute(value, ("dp", "tensor"), pairs))
        return value

    cot_of = [cotangent] + [swap(cotangent, 4 * h) for h in range(1, high_n)]
    weight_core = swap(gate_weight, 1)

    def both(h, same, other):
        value = jnp.concatenate([product(cot_of[h], same), product(cot_of[h], other)], axis=1)
        return swap(value, 4 * h) if h else value

    reduced = [[] for _ in range(z_n)]
    rows = own_rows // early_pieces
    for h in range(high_n):
        for p in range(early_pieces):
            cut = slice(p * rows, (p + 1) * rows)
            reduced[2 * h].append(
                reduce_block(both(h, gate_weight[cut], weight_core[cut]), 2 * h)
            )
    rows = own_rows // x_pieces
    for p in range(x_pieces):
        same = swap(gate_weight[p * rows : (p + 1) * rows], 2)
        other = swap(same, 1)
        for h in range(high_n):
            reduced[2 * h + 1].append(reduce_block(both(h, same, other), 2 * h + 1))

    def whole(parts):
        half = parts[0].shape[1] // 2
        return jnp.concatenate([v[:, :half] for v in parts] + [v[:, half:] for v in parts], axis=1)

    offset = (me // 2) ^ z
    mine = whole(reduced[0])
    for e in range(1, z_n):
        mine = jnp.where(offset == e, whole(reduced[e]), mine)
    input_grad = jnp.where(me % 2 == 0, mine, jnp.roll(mine, own_rows, axis=1))

    coords = jnp.dot(activations, basis, preferred_element_type=jnp.float32).astype(jnp.bfloat16)
    high_rows = coords.shape[1] // high_n
    owned = 0.0
    for h in range(high_n):
        part = lax.dynamic_slice_in_dim(coords, ((me // 4) ^ h) * high_rows, high_rows, 1)
        part = swap(part, 4 * h) if h else part
        owned = owned + lax.dot_general(
            part, cot_of[h], (((0,), (0,)), ((), ())), preferred_element_type=jnp.float32
        )
    for mask in (2, 1):
        half = owned.shape[0] // 2
        upper = (me & mask) != 0
        keep = jnp.where(upper, owned[half:], owned[:half])
        send = jnp.where(upper, owned[:half], owned[half:]).astype(jnp.bfloat16)
        owned = keep + swap(send, mask).astype(jnp.float32)

    total = jnp.sum(owned * owned).reshape(1, 1)
    mask = 1
    while mask < dp_n:
        total = total + swap(total, mask)
        mask *= 2
    mask = 1
    while mask < z_n:
        total = total + lax.ppermute(total, "tensor", [(i, i ^ mask) for i in range(z_n)])
        mask *= 2
    factor = 1.0 / jnp.sqrt(total + norm_epsilon)
    scaled = factor * owned
    new_first = beta_one * first_moment + (1.0 - beta_one) * scaled
    new_second = beta_two * second_moment + (1.0 - beta_two) * scaled * scaled
    first_hat = new_first / (1.0 - beta_one**adam_count)
    second_hat = new_second / (1.0 - beta_two**adam_count)
    direction = (first_hat / (jnp.sqrt(second_hat) + adam_epsilon)).astype(jnp.bfloat16)
    mask = 1
    while mask < dp_n:
        got = swap(direction, mask)
        upper = (me & mask) != 0
        direction = jnp.concatenate(
            [jnp.where(upper, got, direction), jnp.where(upper, direction, got)], axis=0
        )
        mask *= 2
    basis_rows = lax.dynamic_slice_in_dim(basis, me * own_rows, own_rows, 0)
    weight_step = jnp.dot(
        basis_rows, direction, preferred_element_type=jnp.float32
    ).astype(jnp.bfloat16)
    return (input_grad, weight_step, new_first, new_second)


def solution(mesh):
    dp_n, z_n = mesh.shape["dp"], mesh.shape["tensor"]
    assert dp_n == 2 * z_n and dp_n % 4 == 0
    in_specs = (
        P("dp", None),
        P("dp", "tensor"),
        P("dp", "tensor"),
        P(),
        P("dp", "tensor"),
        P("dp", "tensor"),
    )
    out_specs = (P("dp", "tensor"), P("dp", "tensor"), P("dp", "tensor"), P("dp", "tensor"))
    return jax.shard_map(
        functools.partial(on_device, dp_n, z_n),
        mesh=mesh,
        in_specs=in_specs,
        out_specs=out_specs,
        check_vma=False,
    )
```

time: 524 us -> 587 us (1.12)
  the two profiles are of different devices: /device:TPU:7 before, /device:TPU:0 now
where the time goes in v1:
time: 587 us; the launch traced here: 576 us
  waiting for transfers between devices  305 us (52%)
  starting transfers between devices  160 us (27%)
  matrix products  83.2 us (14%)
  other arithmetic  12.1 us (2%)
  local copies, waits for them, and re-layouts  10.1 us (2%)
  between operations  6.19 us (1%)
    ppermute x25, waiting for transfers between devices, swap(): return lax.ppermute(value, 'dp', [(i, i ^ mask) for i in range(dp_n)])  169 us
    ppermute x36, waiting for transfers between devices, reduce_block(): value = add(value, lax.ppermute(value, ('dp', 'tensor'), pairs))  135 us
    ppermute x25, starting transfers between devices, swap(): return lax.ppermute(value, 'dp', [(i, i ^ mask) for i in range(dp_n)])  95.7 us
    dot_general x24, matrix products, product(): lax.dot_general(left, right, (((1,), (1,)), ((), ())), preferred_element_...  71.3 us
    ppermute x36, starting transfers between devices, reduce_block(): value = add(value, lax.ppermute(value, ('dp', 'tensor'), pairs))  57.7 us
  transfers between devices with their start and end apart: 63, of which 21 were waited for; matrix products, arithmetic and copies ran while one was open for 17% of the time, Pallas kernels for 0%

profile of v1, /device:TPU:0, one launch (start us, length us, event | category | flops | bytes accessed | tf_op | source)
XLA Modules:
  0.0 576.4 jit_solution(10286501094617309019)
XLA Ops:
  3.7 6.9 %fusion.52 = (bf16[256,3584]{1,0:T(8,128)(2,1)}, bf16[256,3584]{1,0:T(8,128)(2,1)}, bf16[256,3584]{1,0:T(8,128)(2,1)}, bf16[256,3584]{1,0:T(8,128)(2,1)}) fusion(bf16[1024,3584]{1,0:T(8,128)(2,1)} %param.8), kind=kLoop, calls=%fused_computation.138 | loop fusion | bytes 14680064 | tf_op jit(solution)/shard_map/slice | solution.py:66
  10.6 4.9 collective-permute-start.19
  15.5 5.7 collective-permute-start.13
  21.2 5.7 collective-permute-start.7
  31.3 5.4 fusion.23
  39.5 19.0 %collective-permute-done.19 = bf16[256,3584]{1,0:T(8,128)(2,1)} collective-permute-done((bf16[256,3584]{1,0:T(8,128)(2,1)}, bf16[256,3584]{1,0:T(8,128)(2,1)}, u32[]{:S(2)}, u32[]{:S(2)}) %collective-permute-start.19) | collective-permute-done | bytes 1835040 | tf_op jit(solution)/shard_map/ppermute | solution.py:35
  61.2 36.7 %collective-permute-done.13 = bf16[256,3584]{1,0:T(8,128)(2,1)} collective-permute-done((bf16[256,3584]{1,0:T(8,128)(2,1)}, bf16[256,3584]{1,0:T(8,128)(2,1)}, u32[]{:S(2)}, u32[]{:S(2)}) %collective-permute-start.13) | collective-permute-done | bytes 1835040 | tf_op jit(solution)/shard_map/ppermute | solution.py:35
  101.9 35.2 %collective-permute-done.7 = bf16[256,3584]{1,0:T(8,128)(2,1)} collective-permute-done((bf16[256,3584]{1,0:T(8,128)(2,1)}, bf16[256,3584]{1,0:T(8,128)(2,1)}, u32[]{:S(2)}, u32[]{:S(2)}) %collective-permute-start.7) | collective-permute-done | bytes 1835040 | tf_op jit(solution)/shard_map/ppermute | solution.py:35
  139.8 36.2 %collective-permute-done.1 = bf16[256,3584]{1,0:T(8,128)(2,1)} collective-permute-done((bf16[256,3584]{1,0:T(8,128)(2,1)}, bf16[256,3584]{1,0:T(8,128)(2,1)}, u32[]{:S(2)}, u32[]{:S(2)}) %collective-permute-start.1) | collective-permute-done | bytes 1835040 | tf_op jit(solution)/shard_map/ppermute | solution.py:35
  182.2 3.8 convolution_convert_fusion.10
  190.8 4.1 convolution_convert_fusion.12
  212.6 3.8 convolution_convert_fusion.16
  222.2 4.1 fusion.26
  226.3 4.1 fusion.20
  234.4 8.5 %collective-permute-done.37 = bf16[512,512]{0,1:T(8,128)(2,1)S(1)} collective-permute-done((bf16[512,512]{0,1:T(8,128)(2,1)S(1)}, bf16[512,512]{0,1:T(8,128)(2,1)S(1)}, u32[]{:S(2)}, u32[]{:S(2)}) %collective-permute-start.37) | collective-permute-done | bytes 524320 | tf_op jit(solution)/shard_map/ppermute | solution.py:46
  251.9 5.8 %collective-permute-start.57 = (f32[1,1]{1,0:T(1,128)}, f32[1,1]{1,0:T(1,128)}, u32[]{:S(2)}, u32[]{:S(2)}) collective-permute-start(f32[1,1]{1,0:T(1,128)} %add.206), channel_id=1, source_target_pairs={{0,16},{4,20},{8,24},{12,28},{16,0},{20,4},{24,8},{28,12},{1,17},{... | collective-permute-start | bytes 20 | tf_op jit(solution)/shard_map/ppermute | solution.py:35
  274.3 6.8 %collective-permute-done.34 = bf16[512,512]{0,1:T(8,128)(2,1)S(1)} collective-permute-done((bf16[512,512]{0,1:T(8,128)(2,1)S(1)}, bf16[512,512]{0,1:T(8,128)(2,1)S(1)}, u32[]{:S(2)}, u32[]{:S(2)}) %collective-permute-start.34) | collective-permute-done | bytes 524320 | tf_op jit(solution)/shard_map/ppermute | solution.py:46
  282.6 4.4 collective-permute-start.22
  288.6 10.2 %collective-permute-done.22 = bf16[512,512]{0,1:T(8,128)(2,1)S(1)} collective-permute-done((bf16[512,512]{0,1:T(8,128)(2,1)S(1)}, bf16[512,512]{0,1:T(8,128)(2,1)S(1)}, u32[]{:S(2)}, u32[]{:S(2)}) %collective-permute-start.22) | collective-permute-done | bytes 524320 | tf_op jit(solution)/shard_map/ppermute | solution.py:46
  298.8 5.5 collective-permute-start.16
  306.2 14.1 %collective-permute-start.10 = (bf16[512,512]{0,1:T(8,128)(2,1)S(1)}, bf16[512,512]{0,1:T(8,128)(2,1)S(1)}, u32[]{:S(2)}, u32[]{:S(2)}) collective-permute-start(bf16[512,512]{0,1:T(8,128)(2,1)S(1)} %collective-permute-done.9), channel_id=1, source_target_pairs={{0,1},{4,5},{8,9},{11,10},{12,13},{15,14},{16,17},{19,18},{20,21},... | collective-permute-start | bytes 1572872 | tf_op jit(solution)/shard_map/ppermute | solution.py:46
  322.8 9.8 %collective-permute-done.10 = bf16[512,512]{0,1:T(8,128)(2,1)S(1)} collective-permute-done((bf16[512,512]{0,1:T(8,128)(2,1)S(1)}, bf16[512,512]{0,1:T(8,128)(2,1)S(1)}, u32[]{:S(2)}, u32[]{:S(2)}) %collective-permute-start.10) | collective-permute-done | bytes 524320 | tf_op jit(solution)/shard_map/ppermute | solution.py:46
  334.3 7.4 %collective-permute-done.4 = bf16[512,512]{0,1:T(8,128)(2,1)S(1)} collective-permute-done((bf16[512,512]{0,1:T(8,128)(2,1)S(1)}, bf16[512,512]{0,1:T(8,128)(2,1)S(1)}, u32[]{:S(2)}, u32[]{:S(2)}) %collective-permute-start.4) | collective-permute-done | bytes 524320 | tf_op jit(solution)/shard_map/ppermute | solution.py:46
  358.2 4.1 fusion.38
  362.4 58.2 %collective-permute-start.30 = (bf16[512,1024]{0,1:T(8,128)(2,1)S(1)}, bf16[512,1024]{0,1:T(8,128)(2,1)S(1)}, u32[]{:S(2)}, u32[]{:S(2)}) collective-permute-start(bf16[512,1024]{0,1:T(8,128)(2,1)S(1)} %pad_maximum_fusion.1), channel_id=1, source_target_pairs={{0,16},{4,20},{8,24},{12,28},{16,0},{20,4},{24,8},{28,12},{1,17},{... | collective-permute-start | bytes 3145736 | tf_op jit(solution)/shard_map/ppermute | solution.py:35
  420.6 4.1 fusion.32
  426.0 18.7 %collective-permute-done.30 = bf16[512,1024]{0,1:T(8,128)(2,1)S(1)} collective-permute-done((bf16[512,1024]{0,1:T(8,128)(2,1)S(1)}, bf16[512,1024]{0,1:T(8,128)(2,1)S(1)}, u32[]{:S(2)}, u32[]{:S(2)}) %collective-permute-start.30) | collective-permute-done | bytes 1048608 | tf_op jit(solution)/shard_map/ppermute | solution.py:35
  447.3 15.6 %collective-permute-done.26 = bf16[512,1024]{0,1:T(8,128)(2,1)S(1)} collective-permute-done((bf16[512,1024]{0,1:T(8,128)(2,1)S(1)}, bf16[512,1024]{0,1:T(8,128)(2,1)S(1)}, u32[]{:S(2)}, u32[]{:S(2)}) %collective-permute-start.26) | collective-permute-done | bytes 1048608 | tf_op jit(solution)/shard_map/ppermute | solution.py:35
  465.8 17.2 %collective-permute-done.27 = bf16[512,1024]{0,1:T(8,128)(2,1)S(1)} collective-permute-done((bf16[512,1024]{0,1:T(8,128)(2,1)S(1)}, bf16[512,1024]{0,1:T(8,128)(2,1)S(1)}, u32[]{:S(2)}, u32[]{:S(2)}) %collective-permute-start.27) | collective-permute-done | bytes 1048608 | tf_op jit(solution)/shard_map/ppermute | solution.py:46
  487.3 6.2 %convolution_convert_fusion = bf16[1024,3584]{1,0:T(8,128)(2,1)} fusion(bf16[128,3584]{1,0:T(8,128)(2,1)S(1)} %get-tuple-element.20, bf16[128,3584]{1,0:T(8,128)(2,1)S(1)} %get-tuple-element.19, bf16[8192,256]{1,0:T(8,128)(2,1)} %param.9, s32[]{:T(128)S(6)} %select_n.116), kind=kOutput, calls=%fused_computation | convolution fusion | flops 1886388224 | bytes 9699332 | tf_op jit(solution)/shard_map/dot_general | solution.py:122
  495.6 57.8 %collective-permute-done.48 = bf16[512,1024]{0,1:T(8,128)(2,1)S(1)} collective-permute-done((bf16[512,1024]{0,1:T(8,128)(2,1)S(1)}, bf16[512,1024]{0,1:T(8,128)(2,1)S(1)}, u32[]{:S(2)}, u32[]{:S(2)}) %collective-permute-start.48) | collective-permute-done | bytes 1048608 | tf_op jit(solution)/shard_map/ppermute | solution.py:46
  553.7 16.8 %collective-permute-done.51 = bf16[512,1024]{0,1:T(8,128)(2,1)S(1)} collective-permute-done((bf16[512,1024]{0,1:T(8,128)(2,1)S(1)}, bf16[512,1024]{0,1:T(8,128)(2,1)S(1)}, u32[]{:S(2)}, u32[]{:S(2)}) %collective-permute-start.51) | collective-permute-done | bytes 1048608 | tf_op jit(solution)/shard_map/ppermute | solution.py:46
  (221 shorter events, 123.4 us)
Async XLA Ops:
  0.7 178.6 %collective-permute-start = (bf16[512,3584]{1,0:T(8,128)(2,1)}, bf16[512,3584]{1,0:T(8,128)(2,1)}, u32[]{:S(2)}, u32[]{:S(2)}) collective-permute-start(bf16[512,3584]{1,0:T(8,128)(2,1)} %param.7), channel_id=1, source_target_pairs={{0,16},{4,20},{8,24},{12,28},{16,0},{20,4},{24,8},{28,12},{1,17},{... | collective-permute-start | bytes 11010056 | tf_op jit(solution)/shard_map/ppermute | solution.py:35
  10.6 47.9 %collective-permute-start.19 = (bf16[256,3584]{1,0:T(8,128)(2,1)}, bf16[256,3584]{1,0:T(8,128)(2,1)}, u32[]{:S(2)}, u32[]{:S(2)}) collective-permute-start(bf16[256,3584]{1,0:T(8,128)(2,1)} %get-tuple-element.13), channel_id=1, source_target_pairs={{0,8},{4,12},{8,0},{12,4},{16,24},{20,28},{24,16},{28,20},{1,9},{5... | collective-permute-start | bytes 5505032 | tf_op jit(solution)/shard_map/ppermute | solution.py:35
  15.5 82.3 %collective-permute-start.13 = (bf16[256,3584]{1,0:T(8,128)(2,1)}, bf16[256,3584]{1,0:T(8,128)(2,1)}, u32[]{:S(2)}, u32[]{:S(2)}) collective-permute-start(bf16[256,3584]{1,0:T(8,128)(2,1)} %get-tuple-element.14), channel_id=1, source_target_pairs={{0,8},{4,12},{8,0},{12,4},{16,24},{20,28},{24,16},{28,20},{1,9},{5... | collective-permute-start | bytes 5505032 | tf_op jit(solution)/shard_map/ppermute | solution.py:35
  21.2 115.9 %collective-permute-start.7 = (bf16[256,3584]{1,0:T(8,128)(2,1)}, bf16[256,3584]{1,0:T(8,128)(2,1)}, u32[]{:S(2)}, u32[]{:S(2)}) collective-permute-start(bf16[256,3584]{1,0:T(8,128)(2,1)} %get-tuple-element.15), channel_id=1, source_target_pairs={{0,8},{4,12},{8,0},{12,4},{16,24},{20,28},{24,16},{28,20},{1,9},{5... | collective-permute-start | bytes 5505032 | tf_op jit(solution)/shard_map/ppermute | solution.py:35
  27.0 149.0 %collective-permute-start.1 = (bf16[256,3584]{1,0:T(8,128)(2,1)}, bf16[256,3584]{1,0:T(8,128)(2,1)}, u32[]{:S(2)}, u32[]{:S(2)}) collective-permute-start(bf16[256,3584]{1,0:T(8,128)(2,1)} %get-tuple-element.16), channel_id=1, source_target_pairs={{0,8},{4,12},{8,0},{12,4},{16,24},{20,28},{24,16},{28,20},{1,9},{5... | collective-permute-start | bytes 5505032 | tf_op jit(solution)/shard_map/ppermute | solution.py:35
  58.5 293.8 %collective-permute-start.25 = (bf16[1024,3584]{1,0:T(8,128)(2,1)S(1)}, bf16[1024,3584]{1,0:T(8,128)(2,1)S(1)}, u32[]{:S(2)}, u32[]{:S(2)}) collective-permute-start(bf16[1024,3584]{1,0:T(8,128)(2,1)S(1)} %bitcast.48), channel_id=1, source_target_pairs={{0,4},{4,0},{8,12},{12,8},{16,20},{20,16},{24,28},{28,24},{1,5},{5... | collective-permute-start | bytes 22020104 | tf_op jit(solution)/shard_map/ppermute | solution.py:35
  97.8 80.8 %collective-permute-start.52 = (bf16[512,128]{1,0:T(8,128)(2,1)S(1)}, bf16[512,128]{1,0:T(8,128)(2,1)S(1)}, u32[]{:S(2)}, u32[]{:S(2)}) collective-permute-start(bf16[512,128]{1,0:T(8,128)(2,1)S(1)} %constant_dynamic-slice_fusion), channel_id=1, source_target_pairs={{0,16},{4,20},{8,24},{12,28},{16,0},{20,4},{24,8},{28,12},{1,17},{... | collective-permute-start | bytes 393224 | tf_op jit(solution)/shard_map/ppermute | solution.py:35
  137.2 48.8 %collective-permute-start.20 = (bf16[256,3584]{1,0:T(8,128)(2,1)}, bf16[256,3584]{1,0:T(8,128)(2,1)S(1)}, u32[]{:S(2)}, u32[]{:S(2)}) collective-permute-start(bf16[256,3584]{1,0:T(8,128)(2,1)} %collective-permute-done.19), channel_id=1, source_target_pairs={{0,4},{4,0},{8,12},{12,8},{16,20},{20,16},{24,28},{28,24},{1,5},{5... | collective-permute-start | bytes 5505032 | tf_op jit(solution)/shard_map/ppermute | solution.py:35
  178.7 28.0 %collective-permute-start.8 = (bf16[256,3584]{1,0:T(8,128)(2,1)}, bf16[256,3584]{1,0:T(8,128)(2,1)S(1)}, u32[]{:S(2)}, u32[]{:S(2)}) collective-permute-start(bf16[256,3584]{1,0:T(8,128)(2,1)} %collective-permute-done.7), channel_id=1, source_target_pairs={{0,4},{4,0},{8,12},{12,8},{16,20},{20,16},{24,28},{28,24},{1,5},{5... | collective-permute-start | bytes 5505032 | tf_op jit(solution)/shard_map/ppermute | solution.py:35
  179.2 37.1 %collective-permute-start.2 = (bf16[256,3584]{1,0:T(8,128)(2,1)}, bf16[256,3584]{1,0:T(8,128)(2,1)S(1)}, u32[]{:S(2)}, u32[]{:S(2)}) collective-permute-start(bf16[256,3584]{1,0:T(8,128)(2,1)} %collective-permute-done.1), channel_id=1, source_target_pairs={{0,4},{4,0},{8,12},{12,8},{16,20},{20,16},{24,28},{28,24},{1,5},{5... | collective-permute-start | bytes 5505032 | tf_op jit(solution)/shard_map/ppermute | solution.py:35
  185.9 44.5 %collective-permute-start.53 = (bf16[64,3584]{1,0:T(8,128)(2,1)S(1)}, bf16[64,3584]{1,0:T(8,128)(2,1)S(1)}, u32[]{:S(2)}, u32[]{:S(2)}) collective-permute-start(bf16[64,3584]{1,0:T(8,128)(2,1)S(1)} %select_convert_fusion), channel_id=1, source_target_pairs={{0,8},{4,12},{8,0},{12,4},{16,24},{20,28},{24,16},{28,20},{1,9},{5... | collective-permute-start | bytes 1376264 | tf_op jit(solution)/shard_map/ppermute | solution.py:35
  194.9 37.0 %collective-permute-start.43 = (bf16[512,512]{0,1:T(8,128)(2,1)S(1)}, bf16[512,512]{0,1:T(8,128)(2,1)S(1)}, u32[]{:S(2)}, u32[]{:S(2)}) collective-permute-start(bf16[512,512]{0,1:T(8,128)(2,1)S(1)} %pad_maximum_fusion.12), channel_id=1, source_target_pairs={{0,1},{3,2},{4,5},{7,6},{11,10},{15,14},{16,17},{20,21},{24,25},{2... | collective-permute-start | bytes 1572872 | tf_op jit(solution)/shard_map/ppermute | solution.py:46
  206.7 74.6 %collective-permute-start.21 = (bf16[512,512]{0,1:T(8,128)(2,1)S(1)}, bf16[512,512]{0,1:T(8,128)(2,1)S(1)}, u32[]{:S(2)}, u32[]{:S(2)}) collective-permute-start(bf16[512,512]{0,1:T(8,128)(2,1)S(1)} %pad_maximum_fusion.8), channel_id=1, source_target_pairs={{0,16},{4,20},{8,24},{12,28},{16,0},{20,4},{24,8},{28,12},{1,17},{... | collective-permute-start | bytes 1572872 | tf_op jit(solution)/shard_map/ppermute | solution.py:35
  231.9 56.0 %collective-permute-start.15 = (bf16[512,512]{0,1:T(8,128)(2,1)S(1)}, bf16[512,512]{0,1:T(8,128)(2,1)S(1)}, u32[]{:S(2)}, u32[]{:S(2)}) collective-permute-start(bf16[512,512]{0,1:T(8,128)(2,1)S(1)} %pad_maximum_fusion.7), channel_id=1, source_target_pairs={{0,16},{4,20},{8,24},{12,28},{16,0},{20,4},{24,8},{28,12},{1,17},{... | collective-permute-start | bytes 1572872 | tf_op jit(solution)/shard_map/ppermute | solution.py:35
  232.7 72.7 %collective-permute-start.9 = (bf16[512,512]{0,1:T(8,128)(2,1)S(1)}, bf16[512,512]{0,1:T(8,128)(2,1)S(1)}, u32[]{:S(2)}, u32[]{:S(2)}) collective-permute-start(bf16[512,512]{0,1:T(8,128)(2,1)S(1)} %pad_maximum_fusion.6), channel_id=1, source_target_pairs={{0,16},{4,20},{8,24},{12,28},{16,0},{20,4},{24,8},{28,12},{1,17},{... | collective-permute-start | bytes 1572872 | tf_op jit(solution)/shard_map/ppermute | solution.py:35
  298.8 21.5 %collective-permute-start.16 = (bf16[512,512]{0,1:T(8,128)(2,1)S(1)}, bf16[512,512]{0,1:T(8,128)(2,1)S(1)}, u32[]{:S(2)}, u32[]{:S(2)}) collective-permute-start(bf16[512,512]{0,1:T(8,128)(2,1)S(1)} %collective-permute-done.15), channel_id=1, source_target_pairs={{0,1},{4,5},{8,9},{11,10},{12,13},{15,14},{16,17},{19,18},{20,21},... | collective-permute-start | bytes 1572872 | tf_op jit(solution)/shard_map/ppermute | solution.py:46
  305.5 28.0 %collective-permute-start.35 = (bf16[512,512]{0,1:T(8,128)(2,1)S(1)}, bf16[512,512]{0,1:T(8,128)(2,1)S(1)}, u32[]{:S(2)}, u32[]{:S(2)}) collective-permute-start(bf16[512,512]{0,1:T(8,128)(2,1)S(1)} %add_convert_fusion.23), channel_id=1, source_target_pairs={{2,1},{6,5},{10,9},{14,13},{17,18},{21,22},{25,26},{29,30}} | collective-permute-start | bytes 1572872 | tf_op jit(solution)/shard_map/ppermute | solution.py:46
  306.2 26.4 %collective-permute-start.10 = (bf16[512,512]{0,1:T(8,128)(2,1)S(1)}, bf16[512,512]{0,1:T(8,128)(2,1)S(1)}, u32[]{:S(2)}, u32[]{:S(2)}) collective-permute-start(bf16[512,512]{0,1:T(8,128)(2,1)S(1)} %collective-permute-done.9), channel_id=1, source_target_pairs={{0,1},{4,5},{8,9},{11,10},{12,13},{15,14},{16,17},{19,18},{20,21},... | collective-permute-start | bytes 1572872 | tf_op jit(solution)/shard_map/ppermute | solution.py:46
  320.3 21.4 %collective-permute-start.4 = (bf16[512,512]{0,1:T(8,128)(2,1)S(1)}, bf16[512,512]{0,1:T(8,128)(2,1)S(1)}, u32[]{:S(2)}, u32[]{:S(2)}) collective-permute-start(bf16[512,512]{0,1:T(8,128)(2,1)S(1)} %collective-permute-done.3), channel_id=1, source_target_pairs={{0,1},{4,5},{8,9},{11,10},{12,13},{15,14},{16,17},{19,18},{20,21},... | collective-permute-start | bytes 1572872 | tf_op jit(solution)/shard_map/ppermute | solution.py:46
  321.8 20.7 %collective-permute-start.61 = (bf16[64,3584]{1,0:T(8,128)(2,1)S(1)}, bf16[64,3584]{1,0:T(8,128)(2,1)S(1)}, u32[]{:S(2)}, u32[]{:S(2)}) collective-permute-start(bf16[64,3584]{1,0:T(8,128)(2,1)S(1)} %pad_maximum_fusion.13), channel_id=1, source_target_pairs={{0,8},{4,12},{8,0},{12,4},{16,24},{20,28},{24,16},{28,20},{1,9},{5... | collective-permute-start | bytes 1376264 | tf_op jit(solution)/shard_map/ppermute | solution.py:35
  347.0 117.4 %collective-permute-start.62 = (bf16[128,3584]{1,0:T(8,128)(2,1)S(1)}, bf16[128,3584]{1,0:T(8,128)(2,1)S(1)}, u32[]{:S(2)}, u32[]{:S(2)}) collective-permute-start(bf16[128,3584]{1,0:T(8,128)(2,1)S(1)} %pad_maximum_fusion.4), channel_id=1, source_target_pairs={{0,16},{4,20},{8,24},{12,28},{16,0},{20,4},{24,8},{28,12},{1,17},{... | collective-permute-start | bytes 2752520 | tf_op jit(solution)/shard_map/ppermute | solution.py:35
  354.5 70.4 %collective-permute-start.46 = (bf16[512,1024]{0,1:T(8,128)(2,1)S(1)}, bf16[512,1024]{0,1:T(8,128)(2,1)S(1)}, u32[]{:S(2)}, u32[]{:S(2)}) collective-permute-start(bf16[512,1024]{0,1:T(8,128)(2,1)S(1)} %pad_maximum_fusion.2), channel_id=1, source_target_pairs={{3,2},{7,6},{8,9},{11,10},{12,13},{15,14},{16,17},{19,18},{20,21},... | collective-permute-start | bytes 3145736 | tf_op jit(solution)/shard_map/ppermute | solution.py:46
  357.4 88.6 %collective-permute-start.49 = (bf16[512,1024]{0,1:T(8,128)(2,1)S(1)}, bf16[512,1024]{0,1:T(8,128)(2,1)S(1)}, u32[]{:S(2)}, u32[]{:S(2)}) collective-permute-start(bf16[512,1024]{0,1:T(8,128)(2,1)S(1)} %pad_maximum_fusion.3), channel_id=1, source_target_pairs={{3,2},{7,6},{8,9},{11,10},{12,13},{15,14},{16,17},{19,18},{20,21},... | collective-permute-start | bytes 3145736 | tf_op jit(solution)/shard_map/ppermute | solution.py:46
  362.4 82.3 %collective-permute-start.30 = (bf16[512,1024]{0,1:T(8,128)(2,1)S(1)}, bf16[512,1024]{0,1:T(8,128)(2,1)S(1)}, u32[]{:S(2)}, u32[]{:S(2)}) collective-permute-start(bf16[512,1024]{0,1:T(8,128)(2,1)S(1)} %pad_maximum_fusion.1), channel_id=1, source_target_pairs={{0,16},{4,20},{8,24},{12,28},{16,0},{20,4},{24,8},{28,12},{1,17},{... | collective-permute-start | bytes 3145736 | tf_op jit(solution)/shard_map/ppermute | solution.py:35
  424.8 38.1 %collective-permute-start.26 = (bf16[512,1024]{0,1:T(8,128)(2,1)S(1)}, bf16[512,1024]{0,1:T(8,128)(2,1)S(1)}, u32[]{:S(2)}, u32[]{:S(2)}) collective-permute-start(bf16[512,1024]{0,1:T(8,128)(2,1)S(1)} %pad_maximum_fusion), channel_id=1, source_target_pairs={{0,16},{4,20},{8,24},{12,28},{16,0},{20,4},{24,8},{28,12},{1,17},{... | collective-permute-start | bytes 3145736 | tf_op jit(solution)/shard_map/ppermute | solution.py:35
  425.3 58.8 %collective-permute-start.47 = (bf16[512,1024]{0,1:T(8,128)(2,1)S(1)}, bf16[512,1024]{0,1:T(8,128)(2,1)S(1)}, u32[]{:S(2)}, u32[]{:S(2)}) collective-permute-start(bf16[512,1024]{0,1:T(8,128)(2,1)S(1)} %add_convert_fusion.5), channel_id=1, source_target_pairs={{2,1},{6,5},{10,9},{14,13},{17,18},{21,22},{25,26},{29,30}} | collective-permute-start | bytes 3145736 | tf_op jit(solution)/shard_map/ppermute | solution.py:46
  446.4 39.3 %collective-permute-start.50 = (bf16[512,1024]{0,1:T(8,128)(2,1)S(1)}, bf16[512,1024]{0,1:T(8,128)(2,1)S(1)}, u32[]{:S(2)}, u32[]{:S(2)}) collective-permute-start(bf16[512,1024]{0,1:T(8,128)(2,1)S(1)} %add_convert_fusion.2), channel_id=1, source_target_pairs={{2,1},{6,5},{10,9},{14,13},{17,18},{21,22},{25,26},{29,30}} | collective-permute-start | bytes 3145736 | tf_op jit(solution)/shard_map/ppermute | solution.py:46
  465.0 28.4 %collective-permute-start.32 = (bf16[512,1024]{0,1:T(8,128)(2,1)S(1)}, bf16[512,1024]{0,1:T(8,128)(2,1)S(1)}, u32[]{:S(2)}, u32[]{:S(2)}) collective-permute-start(bf16[512,1024]{0,1:T(8,128)(2,1)S(1)} %add_convert_fusion.8), channel_id=1, source_target_pairs={{1,2},{5,6},{9,10},{13,14},{18,17},{22,21},{26,25},{30,29}} | collective-permute-start | bytes 3145736 | tf_op jit(solution)/shard_map/ppermute | solution.py:46
  484.4 69.0 %collective-permute-start.48 = (bf16[512,1024]{0,1:T(8,128)(2,1)S(1)}, bf16[512,1024]{0,1:T(8,128)(2,1)S(1)}, u32[]{:S(2)}, u32[]{:S(2)}) collective-permute-start(bf16[512,1024]{0,1:T(8,128)(2,1)S(1)} %add_convert_fusion.4), channel_id=1, source_target_pairs={{1,0},{5,4},{26,27},{30,31}} | collective-permute-start | bytes 3145736 | tf_op jit(solution)/shard_map/ppermute | solution.py:46
  486.0 84.5 %collective-permute-start.51 = (bf16[512,1024]{0,1:T(8,128)(2,1)S(1)}, bf16[512,1024]{0,1:T(8,128)(2,1)S(1)}, u32[]{:S(2)}, u32[]{:S(2)}) collective-permute-start(bf16[512,1024]{0,1:T(8,128)(2,1)S(1)} %add_convert_fusion.1), channel_id=1, source_target_pairs={{1,0},{5,4},{26,27},{30,31}} | collective-permute-start | bytes 3145736 | tf_op jit(solution)/shard_map/ppermute | solution.py:46
  493.8 77.2 %collective-permute-start.33 = (bf16[512,1024]{0,1:T(8,128)(2,1)S(1)}, bf16[512,1024]{0,1:T(8,128)(2,1)S(1)}, u32[]{:S(2)}, u32[]{:S(2)}) collective-permute-start(bf16[512,1024]{0,1:T(8,128)(2,1)S(1)} %add_convert_fusion.7), channel_id=1, source_target_pairs={{10,11},{14,15},{17,16},{21,20}} | collective-permute-start | bytes 3145736 | tf_op jit(solution)/shard_map/ppermute | solution.py:46
  494.8 76.6 %collective-permute-start.29 = (bf16[512,1024]{0,1:T(8,128)(2,1)S(1)}, bf16[512,1024]{0,1:T(8,128)(2,1)S(1)}, u32[]{:S(2)}, u32[]{:S(2)}) collective-permute-start(bf16[512,1024]{0,1:T(8,128)(2,1)S(1)} %add_convert_fusion.10), channel_id=1, source_target_pairs={{10,11},{14,15},{17,16},{21,20}} | collective-permute-start | bytes 3145736 | tf_op jit(solution)/shard_map/ppermute | solution.py:46
  (38 other events, 419.5 us)

commit v2 on v1

--- a/solution.py
+++ b/solution.py
@@ -3,6 +3,8 @@
 import jax
 import jax.numpy as jnp
 from jax import lax
+from jax.experimental import pallas as pl
+from jax.experimental.pallas import tpu as pltpu
 from jax.sharding import PartitionSpec as P
 
 beta_one = 0.9
@@ -125,9 +127,383 @@
     return (input_grad, weight_step, new_first, new_second)
 
 
+def moments(factor, owned, first, second):
+    scaled = factor * owned
+    new_first = beta_one * first + (1.0 - beta_one) * scaled
+    new_second = beta_two * second + (1.0 - beta_two) * scaled * scaled
+    first_hat = new_first / (1.0 - beta_one**adam_count)
+    second_hat = new_second / (1.0 - beta_two**adam_count)
+    direction = (first_hat / (jnp.sqrt(second_hat) + adam_epsilon)).astype(jnp.bfloat16)
+    return new_first, new_second, direction
+
+
+ORDER = (
+    (0, 0), (0, 1), (0, 2), (0, 3), (1, 0), (1, 1), (2, 0), (2, 1),
+    (2, 2), (1, 2), (2, 3), (3, 0), (3, 1), (1, 3), (3, 2), (3, 3),
+)
+CHUNKS = 4
+LAG = 2
+
+
+def exchange_kernel(
+    z_n, cot_ref, w_ref, coords_ref, first_ref, second_ref,
+    grad_ref, new_first_ref, new_second_ref, dirs_out_ref,
+    cots, ws, parts, z_got, fin_got, coords_got, proj, proj_send, proj_got, sums, zsums, dirs,
+    local_sem, cot_send, cot_recv, w_send, w_recv, ret_send, ret_recv, z_send, z_recv,
+    fin_send, fin_recv, co_send, co_recv, px_send, px_recv, s_send, s_recv, t_send, t_recv,
+    d_send, d_recv,
+):
+    me = lax.axis_index("dp")
+    z = lax.axis_index("tensor")
+    core = me % 2
+    x_bit = (me // 2) % 2
+    y_bit = me // 4
+    block = me // 2
+    tokens = cots.shape[1]
+    cols = parts.shape[3]
+    half_tokens = tokens // 2
+
+    def flip(mask):
+        c = 1 - core if mask & 1 else core
+        x = 1 - x_bit if mask & 2 else x_bit
+        y = 1 - y_bit if mask & 4 else y_bit
+        return y * 4 + x * 2 + c
+
+    def remote(src, dst, send, recv, dp, tensor):
+        return pltpu.make_async_remote_copy(
+            src_ref=src, dst_ref=dst, send_sem=send, recv_sem=recv,
+            device_id=(dp, tensor), device_id_type=pl.DeviceIdType.MESH,
+        )
+
+    barrier = pltpu.get_barrier_semaphore()
+    for mask in range(1, 8):
+        pl.semaphore_signal(barrier, inc=1, device_id=(flip(mask), z), device_id_type=pl.DeviceIdType.MESH)
+    for step in range(1, z_n):
+        pl.semaphore_signal(barrier, inc=1, device_id=(me, (z + step) % z_n), device_id_type=pl.DeviceIdType.MESH)
+    local = [
+        pltpu.make_async_copy(cot_ref, cots.at[0], local_sem.at[0]),
+        pltpu.make_async_copy(w_ref, ws.at[0], local_sem.at[1]),
+    ]
+    for copy in local:
+        copy.start()
+    pl.semaphore_wait(barrier, 7 + z_n - 1)
+
+    def w_copy(p):
+        rows = pl.ds(p * cols, cols)
+        return remote(w_ref.at[rows], ws.at[1, rows], w_send.at[p], w_recv.at[p], flip(2), z)
+
+    def y_copy(h):
+        rows = pl.ds(h * half_tokens, half_tokens)
+        return remote(cot_ref.at[rows], cots.at[2, rows], cot_send.at[1 + h], cot_recv.at[1 + h], flip(4), z)
+
+    def forward_copy(h):
+        rows = pl.ds(h * half_tokens, half_tokens)
+        return remote(cots.at[2, rows], cots.at[3, rows], cot_send.at[3 + h], cot_recv.at[3 + h], flip(1), z)
+
+    core_copy = remote(cot_ref, cots.at[1], cot_send.at[0], cot_recv.at[0], flip(1), z)
+
+    high_rows = coords_ref.shape[0] // 4
+
+    def coords_rows(b):
+        return coords_ref.at[pl.ds(pl.multiple_of(b * high_rows, high_rows), high_rows)]
+
+    def coords_copy(m):
+        mask = (m & 1) + 2 * (m & 2)
+        there = flip(mask)
+        b = (there // 4) * 2 + there % 2
+        return remote(coords_rows(b), coords_got.at[m - 1], co_send.at[m - 1], co_recv.at[m - 1], there, z)
+
+    w_copy(0).start()
+    y_copy(0).start()
+    core_copy.start()
+    for m in range(1, 4):
+        coords_copy(m).start()
+    w_copy(1).start()
+    y_copy(1).start()
+    for copy in local:
+        copy.wait()
+
+    def unit(t, w, q):
+        value = lax.dot_general(
+            cots[t], ws[w, pl.ds(pl.multiple_of(q * cols, cols), cols), :],
+            (((1,), (1,)), ((), ())), preferred_element_type=jnp.float32,
+        )
+        rows = pl.ds(pl.multiple_of((t % 2) * tokens, tokens), tokens)
+        parts[w + 4 * (t // 2), q, rows, :] = value.astype(jnp.bfloat16)
+
+    def return_copy(w, q):
+        i = w * CHUNKS + q
+        return remote(parts.at[4 + w, q], parts.at[2 + w, q], ret_send.at[i], ret_recv.at[i], flip(4), z)
+
+    def owner(e):
+        y = 1 - y_bit if e & 2 else y_bit
+        x = 1 - x_bit if e & 1 else x_bit
+        return y * 2 + x
+
+    def accumulate(e, q, slots):
+        def body(i, carry):
+            rows = pl.ds(pl.multiple_of(i * 64, 64), 64)
+            value = parts[e, q, rows, :].astype(jnp.float32)
+            for slot in slots:
+                value = value + z_got[slot, q, rows, :].astype(jnp.float32)
+            parts[e, q, rows, :] = value.astype(jnp.bfloat16)
+            return carry
+        lax.fori_loop(0, 2 * tokens // 64, body, 0)
+
+    def right_copy(e, q):
+        s = owner(e)
+        return remote(parts.at[e, q], z_got.at[s + 1, q], z_send.at[e, q], z_recv.at[s + 1, q], me, lax.rem(z + 1, z_n))
+
+    def left_copy(e, q):
+        s = owner(e)
+        return remote(parts.at[e, q], z_got.at[s, q], z_send.at[e, q], z_recv.at[s, q], me, lax.rem(z + z_n - 1, z_n))
+
+    def z_round(e, q, k):
+        s = owner(e)
+        if k < z_n:
+            @pl.when((z == k - 1) & (z < s))
+            def _():
+                if k > 1:
+                    right_copy(e, q).wait_recv()
+                    accumulate(e, q, [s + 1])
+                right_copy(e, q).start()
+
+            @pl.when((z == z_n - k) & (z > s))
+            def _():
+                if k > 1:
+                    left_copy(e, q).wait_recv()
+                    accumulate(e, q, [s])
+                left_copy(e, q).start()
+        else:
+            @pl.when(z == s)
+            def _():
+                @pl.when(z > 0)
+                def _():
+                    right_copy(e, q).wait_recv()
+                    accumulate(e, q, [s + 1])
+
+                @pl.when(z < z_n - 1)
+                def _():
+                    left_copy(e, q).wait_recv()
+                    accumulate(e, q, [s])
+                fin_copy(e, q).start()
+                grad_ref[:, pl.ds(pl.multiple_of((core * CHUNKS + q) * cols, cols), cols)] = parts[e, q, :tokens, :]
+
+    def fin_copy(e, q):
+        return remote(parts.at[e, q, pl.ds(tokens, tokens)], fin_got.at[q], fin_send.at[q], fin_recv.at[q], flip(1), z)
+
+    def two_units(base, w, q):
+        def body(t, carry):
+            unit(base + t, w, q)
+            return carry
+        lax.fori_loop(0, 2, body, 0)
+
+    def project():
+        b = y_bit * 2 + core
+        own = pl.ds(pl.multiple_of(b * high_rows, high_rows), high_rows)
+        width = cols
+        def body(i, carry):
+            at = pl.ds(pl.multiple_of(i * width, width), width)
+            value = jnp.dot(coords_ref[own, :], cots[0, :, at], preferred_element_type=jnp.float32)
+            for m in range(1, 4):
+                value = value + jnp.dot(coords_got[m - 1], cots[m, :, at], preferred_element_type=jnp.float32)
+            proj[:, at] = value
+            return carry
+        lax.fori_loop(0, proj.shape[1] // width, body, 0)
+
+    out_rows = proj.shape[0] // 2
+    proj_copy = remote(proj_send, proj_got, px_send, px_recv, flip(2), z)
+
+    def send_projected():
+        project()
+        there = pl.ds(pl.multiple_of((1 - x_bit) * out_rows, out_rows), out_rows)
+        proj_send[...] = proj[there, :].astype(jnp.bfloat16)
+        proj_copy.start()
+
+    def sum_copy(m):
+        return remote(sums.at[0], sums.at[m], s_send.at[m], s_recv.at[m], flip(m), z)
+
+    def zsum_copy(step):
+        return remote(zsums.at[0], zsums.at[step], t_send.at[step], t_recv.at[step], me, (z + step) % z_n)
+
+    here = pl.ds(pl.multiple_of(x_bit * out_rows, out_rows), out_rows)
+
+    def send_sums():
+        proj_copy.wait()
+        owned = proj[here, :] + proj_got[...].astype(jnp.float32)
+        proj[here, :] = owned
+        sums[0] = jnp.zeros((8, 128), jnp.float32) + jnp.sum(owned * owned)
+        for m in range(1, 8):
+            sum_copy(m).start()
+
+    def send_zsums():
+        for m in range(1, 8):
+            sum_copy(m).wait()
+        zsums[0] = jnp.sum(sums[...], axis=0)
+        for step in range(1, z_n):
+            zsum_copy(step).start()
+
+    def dir_copy(m):
+        return remote(dirs.at[me], dirs.at[me], d_send.at[m], d_recv.at[m], flip(m), z)
+
+    def send_dirs():
+        for step in range(1, z_n):
+            zsum_copy(step).wait()
+        total = jnp.sum(zsums[...], axis=0)
+        factor = (1.0 / jnp.sqrt(total + norm_epsilon))[0:1, 0:1]
+        one, two, direction = moments(factor, proj[here, :], first_ref[...], second_ref[...])
+        new_first_ref[...] = one
+        new_second_ref[...] = two
+        dirs[me] = direction
+        for m in range(1, 8):
+            dir_copy(m).start()
+
+    def take_dirs():
+        for m in range(1, 8):
+            dir_copy(m).wait()
+        dirs_out_ref[...] = dirs[...].reshape(dirs_out_ref.shape)
+
+    def before(i):
+        e, q = ORDER[i]
+        if i == 0:
+            def body(j, carry):
+                unit(0, 0, j)
+                return carry
+            lax.fori_loop(0, CHUNKS, body, 0)
+            core_copy.wait()
+        if e == 0:
+            unit(1, 0, q)
+        if e == 1:
+            w_copy(q).wait()
+            if q + 2 < CHUNKS:
+                w_copy(q + 2).start()
+            two_units(0, 1, q)
+        if e >= 2:
+            return_copy(e - 2, q).wait()
+
+    def after(i):
+        e, q = ORDER[i]
+        if (e, q) == (1, 0):
+            y_copy(0).wait()
+            forward_copy(0).start()
+        if (e, q) == (1, 1):
+            y_copy(1).wait()
+            forward_copy(1).start()
+            for h in range(2):
+                forward_copy(h).wait_recv()
+            for w, p in ((0, 0), (0, 1), (0, 2), (0, 3), (1, 0), (1, 1)):
+                two_units(2, w, p)
+                return_copy(w, p).start()
+                if (w, p) == (0, 0):
+                    for m in range(1, 4):
+                        coords_copy(m).wait()
+                    send_projected()
+        if e == 1 and q >= 2:
+            two_units(2, 1, q)
+            return_copy(1, q).start()
+
+    stages = {8: send_sums, 10: send_zsums, 12: send_dirs}
+    count = len(ORDER)
+    for i in range(count + LAG * (z_n - 1)):
+        if i < count:
+            before(i)
+            z_round(*ORDER[i], 1)
+            after(i)
+        for k in range(2, z_n + 1):
+            j = i - LAG * (k - 1)
+            if 0 <= j < count:
+                z_round(*ORDER[j], k)
+        if i in stages:
+            stages[i]()
+    take_dirs()
+    for q in range(CHUNKS):
+        fin_copy(0, q).wait()
+        grad_ref[:, pl.ds(pl.multiple_of(((1 - core) * CHUNKS + q) * cols, cols), cols)] = fin_got[q]
+    for h in range(2):
+        forward_copy(h).wait_send()
+    for e, q in ORDER:
+        @pl.when(z != owner(e))
+        def _():
+            right_copy(e, q).wait_send()
+
+
+def exchange(z_n, cotangent, gate_weight, coords, first_moment, second_moment):
+    tokens, hidden = cotangent.shape
+    w_rows = gate_weight.shape[0]
+    cols = w_rows // CHUNKS
+    rank = coords.shape[0]
+    own = first_moment.shape[0]
+    vmem = pl.BlockSpec(memory_space=pltpu.VMEM)
+    hbm = pl.BlockSpec(memory_space=pl.ANY)
+    dma = pltpu.SemaphoreType.DMA
+    bf16, f32 = jnp.bfloat16, jnp.float32
+    flops = 2 * 4 * tokens * 2 * w_rows * hidden
+    return pl.pallas_call(
+        functools.partial(exchange_kernel, z_n),
+        out_shape=[
+            jax.ShapeDtypeStruct((tokens, 2 * w_rows), bf16),
+            jax.ShapeDtypeStruct(first_moment.shape, f32),
+            jax.ShapeDtypeStruct(first_moment.shape, f32),
+            jax.ShapeDtypeStruct((rank, hidden), bf16),
+        ],
+        in_specs=[hbm, hbm, vmem, vmem, vmem],
+        out_specs=[vmem] * 4,
+        scratch_shapes=[
+            pltpu.VMEM((4, tokens, hidden), bf16),
+            pltpu.VMEM((2, w_rows, hidden), bf16),
+            pltpu.VMEM((6, CHUNKS, 2 * tokens, cols), bf16),
+            pltpu.VMEM((z_n + 1, CHUNKS, 2 * tokens, cols), bf16),
+            pltpu.VMEM((CHUNKS, tokens, cols), bf16),
+            pltpu.VMEM((3, rank // 4, tokens), bf16),
+            pltpu.VMEM((2 * own, hidden), f32),
+            pltpu.VMEM((own, hidden), bf16),
+            pltpu.VMEM((own, hidden), bf16),
+            pltpu.VMEM((8, 8, 128), f32),
+            pltpu.VMEM((z_n, 8, 128), f32),
+            pltpu.VMEM((8, own, hidden), bf16),
+            dma((2,)),
+            dma((5,)), dma((5,)),
+            dma((CHUNKS,)), dma((CHUNKS,)),
+            dma((2 * CHUNKS,)), dma((2 * CHUNKS,)),
+            dma((4, CHUNKS)), dma((z_n + 1, CHUNKS)),
+            dma((CHUNKS,)), dma((CHUNKS,)),
+            dma((3,)), dma((3,)),
+            dma, dma,
+            dma((8,)), dma((8,)),
+            dma((z_n,)), dma((z_n,)),
+            dma((8,)), dma((8,)),
+        ],
+        compiler_params=pltpu.CompilerParams(
+            collective_id=0, has_side_effects=True, vmem_limit_bytes=62 * 1024 * 1024
+        ),
+        cost_estimate=pl.CostEstimate(flops=flops, bytes_accessed=24000000, transcendentals=0),
+    )(cotangent, gate_weight, coords, first_moment, second_moment)
+
+
+def on_pairs(z_n, activations, cotangent, gate_weight, basis, first_moment, second_moment):
+    own_rows = gate_weight.shape[0]
+    tokens = activations.shape[0]
+    rank = basis.shape[1]
+    me = lax.axis_index("dp")
+    coords = lax.dot_general(
+        basis, activations, (((0,), (1,)), ((), ())), preferred_element_type=jnp.float32
+    ).astype(jnp.bfloat16)
+    coords = coords.reshape(2, 2, 2, rank // 8, tokens).transpose(0, 2, 1, 3, 4).reshape(rank, tokens)
+    input_grad, new_first, new_second, direction = exchange(
+        z_n, cotangent, gate_weight, coords, first_moment, second_moment
+    )
+    basis_rows = lax.dynamic_slice_in_dim(basis, me * own_rows, own_rows, 0)
+    weight_step = jnp.dot(
+        basis_rows, direction, preferred_element_type=jnp.float32
+    ).astype(jnp.bfloat16)
+    return (input_grad, weight_step, new_first, new_second)
+
+
 def solution(mesh):
     dp_n, z_n = mesh.shape["dp"], mesh.shape["tensor"]
     assert dp_n == 2 * z_n and dp_n % 4 == 0
+    paired = (dp_n, z_n) == (8, 4)
+    body = functools.partial(on_pairs, z_n) if paired else functools.partial(on_device, dp_n, z_n)
     in_specs = (
         P("dp", None),
         P("dp", "tensor"),
@@ -138,7 +514,7 @@
     )
     out_specs = (P("dp", "tensor"), P("dp", "tensor"), P("dp", "tensor"), P("dp", "tensor"))
     return jax.shard_map(
-        functools.partial(on_device, dp_n, z_n),
+        body,
         mesh=mesh,
         in_specs=in_specs,
         out_specs=out_specs,

time: 587 us -> 299 us (0.51)
  the two profiles are of different devices: /device:TPU:0 before, /device:TPU:7 now
where the time goes in v2:
time: 299 us
  Pallas kernels  281 us (94%)
  matrix products  14 us (5%)
  local copies, waits for them, and re-layouts  3.59 us (1%)
    pallas_call x1, Pallas kernels, exchange(): pl.pallas_call(functools.partial(exchange_kernel, z_n), out_shape=[jax.Sh...  281 us
    dot_general x1, matrix products, on_pairs(): lax.dot_general(basis, activations, (((0,), (1,)), ((), ())), preferred_e...  7.04 us
    dot_general x1, matrix products, on_pairs(): jnp.dot(basis_rows, direction, preferred_element_type=jnp.float32)  6.93 us

profile of v2, /device:TPU:7, one launch (start us, length us, event | category | flops | bytes accessed | tf_op | source)
XLA Modules:
  0.0 299.1 jit_solution(13212697676869541667)
XLA Ops:
  0.6 7.0 %convolution_convert_fusion.1 = bf16[256,512]{1,0:T(8,128)(2,1)S(1)} fusion(bf16[8192,256]{1,0:T(8,128)(2,1)} %param.9, bf16[512,8192]{1,0:T(8,128)(2,1)} %param.6), kind=kOutput, calls=%fused_computation.1 | convolution fusion | flops 2147614720 | bytes 12845056 | tf_op jit(solution)/shard_map/dot_general | solution.py:488
  7.7 0.7 copy.10
  8.4 280.9 %shard_map.93 = (bf16[512,2048]{1,0:T(8,128)(2,1)}, f32[32,3584]{1,0:T(8,128)}, f32[32,3584]{1,0:T(8,128)}, bf16[256,3584]{1,0:T(8,128)(2,1)}) custom-call(bf16[512,3584]{1,0:T(8,128)(2,1)} %cot_ref.1, bf16[1024,3584]{1,0:T(8,128)(2,1)} %w_ref.1, bf16[256,512]{1,0:T(8,128)(2,1)} %bitcast.7, f32[32,3584]{1,0:T(8,128)} %first_ref.1, f32[32,3584]{1,0:T(8,128)} %second_ref.1), custom_call_target="tpu_custom_call" | custom-call | flops 30064771072 | bytes 24000000 | tf_op jit(solution)/shard_map/pallas_call | solution.py:441
  289.3 0.0 copy-start
  289.3 6.9 %convolution_convert_fusion = bf16[1024,3584]{1,0:T(8,128)(2,1)} fusion(bf16[256,3584]{1,0:T(8,128)(2,1)} %get-tuple-element.9, bf16[8192,256]{1,0:T(8,128)(2,1)} %param.9, s32[]{:T(128)S(6)} %select_n.3), kind=kOutput, calls=%fused_computation | convolution fusion | flops 1882718208 | bytes 9699332 | tf_op jit(solution)/shard_map/dot_general | solution.py:496
  296.2 0.0 copy-done
  296.2 0.0 copy-start.2
  296.2 0.0 copy-start.1
  296.2 1.3 copy.14
  297.5 0.0 copy-done.2
  297.5 0.8 copy.15
  298.3 0.0 copy-done.1
  298.3 0.8 copy.16
Async XLA Ops:
  289.3 6.9 %copy-start = (bf16[512,2048]{1,0:T(8,128)(2,1)S(1)}, bf16[512,2048]{1,0:T(8,128)(2,1)}, u32[]{:S(2)}) copy-start(bf16[512,2048]{1,0:T(8,128)(2,1)} %get-tuple-element.16) | copy-start | bytes 6291460
  296.2 1.3 copy-start.2
  296.2 2.1 copy-start.1

commit v3 on v2

--- a/solution.py
+++ b/solution.py
@@ -137,12 +137,37 @@
     return new_first, new_second, direction
 
 
+START, OWN, X, Y, BACK, Z, PROJECT, SUMS, ZSUMS, DIRS = range(10)
 ORDER = (
-    (0, 0), (0, 1), (0, 2), (0, 3), (1, 0), (1, 1), (2, 0), (2, 1),
-    (2, 2), (1, 2), (2, 3), (3, 0), (3, 1), (1, 3), (3, 2), (3, 3),
+    (START,), (OWN, 0), (OWN, 1), (Z, 0, 1, 0, 1), (Z, 0, 0, 0, 1),
+    (Z, 0, 0, 0, 2), (Y, 0), (OWN, 2), (OWN, 3), (Z, 0, 3, 0, 1),
+    (BACK, 2, 2, 0), (Z, 0, 3, 0, 2), (Z, 0, 3, 0, 3), (X, 0), (Z, 1, 0, 0, 1),
+    (BACK, 2, 0, 0), (BACK, 2, 1, 0), (Z, 0, 1, 0, 2), (BACK, 2, 3, 0), (Y, 1),
+    (Z, 0, 0, 0, 3), (Z, 0, 2, 0, 1), (X, 1), (Z, 1, 1, 0, 1), (Z, 0, 2, 0, 2),
+    (Z, 2, 2, 0, 1), (BACK, 3, 0, 0), (Z, 2, 0, 0, 1), (Z, 2, 0, 0, 2), (BACK, 3, 1, 0),
+    (Z, 0, 1, 0, 3), (Z, 1, 1, 0, 2), (Z, 0, 3, 0, 4), (Z, 2, 1, 0, 1), (BACK, 2, 2, 1),
+    (Z, 0, 2, 0, 3), (Z, 2, 1, 0, 2), (BACK, 2, 0, 1), (PROJECT,), (Z, 1, 1, 0, 3),
+    (Z, 2, 3, 0, 1), (BACK, 3, 1, 1), (Z, 3, 0, 0, 1), (BACK, 2, 1, 1), (BACK, 3, 0, 1),
+    (Z, 2, 0, 0, 3), (Z, 3, 1, 0, 1), (Z, 3, 1, 0, 2), (X, 2), (BACK, 3, 2, 0),
+    (Z, 1, 2, 0, 1), (BACK, 3, 2, 1), (Z, 3, 0, 0, 2), (Z, 2, 2, 0, 2), (Z, 1, 0, 0, 2),
+    (BACK, 2, 3, 1), (Z, 2, 0, 0, 4), (Z, 2, 2, 1, 1), (Z, 2, 2, 1, 2), (Z, 1, 0, 0, 3),
+    (Z, 2, 2, 1, 3), (Z, 3, 1, 1, 1), (Z, 2, 1, 1, 1), (Z, 3, 1, 1, 2), (Z, 2, 0, 1, 1),
+    (Z, 0, 0, 0, 4), (Z, 2, 1, 1, 2), (Z, 3, 2, 1, 1), (Z, 3, 2, 0, 1), (Z, 2, 3, 1, 1),
+    (Z, 3, 2, 1, 2), (Z, 0, 1, 0, 4), (SUMS,), (Z, 1, 1, 0, 4), (Z, 0, 2, 0, 4),
+    (Z, 3, 2, 0, 2), (Z, 2, 0, 1, 2), (Z, 1, 2, 0, 2), (X, 3), (BACK, 3, 3, 0),
+    (Z, 3, 1, 1, 3), (Z, 2, 1, 0, 3), (Z, 2, 0, 1, 3), (BACK, 3, 3, 1), (Z, 3, 0, 0, 3),
+    (Z, 1, 3, 0, 1), (Z, 3, 2, 0, 3), (Z, 2, 3, 0, 2), (Z, 2, 2, 0, 3), (Z, 2, 2, 1, 4),
+    (ZSUMS,), (Z, 1, 3, 0, 2), (Z, 3, 1, 1, 4), (Z, 2, 3, 1, 2), (Z, 2, 3, 1, 3),
+    (Z, 3, 3, 0, 1), (Z, 3, 3, 0, 2), (Z, 2, 1, 1, 3), (Z, 3, 1, 0, 3), (Z, 3, 3, 1, 1),
+    (Z, 3, 0, 0, 4), (Z, 1, 2, 0, 3), (DIRS,), (Z, 3, 3, 1, 2), (Z, 3, 2, 1, 3),
+    (Z, 2, 3, 1, 4), (Z, 3, 2, 1, 4), (Z, 3, 1, 0, 4), (Z, 3, 2, 0, 4), (Z, 2, 2, 0, 4),
+    (Z, 3, 3, 0, 3), (Z, 3, 0, 1, 1), (Z, 2, 1, 0, 4), (Z, 3, 0, 1, 2), (Z, 1, 2, 0, 4),
+    (Z, 1, 3, 0, 3), (Z, 3, 3, 1, 3), (Z, 2, 1, 1, 4), (Z, 3, 3, 0, 4), (Z, 2, 0, 1, 4),
+    (Z, 2, 3, 0, 3), (Z, 3, 3, 1, 4), (Z, 1, 3, 0, 4), (Z, 3, 0, 1, 3), (Z, 3, 0, 1, 4),
+    (Z, 2, 3, 0, 4), (Z, 1, 0, 0, 4),
 )
 CHUNKS = 4
-LAG = 2
+AHEAD = 3
 
 
 def exchange_kernel(
@@ -159,9 +184,8 @@
     x_bit = (me // 2) % 2
     y_bit = me // 4
     block = me // 2
-    tokens = cots.shape[1]
-    cols = parts.shape[3]
-    half_tokens = tokens // 2
+    half = cots.shape[1] // 2
+    cols = parts.shape[4]
 
     def flip(mask):
         c = 1 - core if mask & 1 else core
@@ -181,8 +205,9 @@
     for step in range(1, z_n):
         pl.semaphore_signal(barrier, inc=1, device_id=(me, (z + step) % z_n), device_id_type=pl.DeviceIdType.MESH)
     local = [
-        pltpu.make_async_copy(cot_ref, cots.at[0], local_sem.at[0]),
-        pltpu.make_async_copy(w_ref, ws.at[0], local_sem.at[1]),
+        pltpu.make_async_copy(cot_ref.at[pl.ds(0, half)], cots.at[0, pl.ds(0, half)], local_sem.at[0]),
+        pltpu.make_async_copy(cot_ref.at[pl.ds(half, half)], cots.at[1, pl.ds(0, half)], local_sem.at[1]),
+        pltpu.make_async_copy(w_ref, ws.at[0], local_sem.at[2]),
     ]
     for copy in local:
         copy.start()
@@ -193,14 +218,15 @@
         return remote(w_ref.at[rows], ws.at[1, rows], w_send.at[p], w_recv.at[p], flip(2), z)
 
     def y_copy(h):
-        rows = pl.ds(h * half_tokens, half_tokens)
-        return remote(cot_ref.at[rows], cots.at[2, rows], cot_send.at[1 + h], cot_recv.at[1 + h], flip(4), z)
+        rows = pl.ds(h * half, half)
+        return remote(cot_ref.at[rows], cots.at[2 + h, pl.ds(0, half)], cot_send.at[2 + h], cot_recv.at[2 + h], flip(4), z)
 
     def forward_copy(h):
-        rows = pl.ds(h * half_tokens, half_tokens)
-        return remote(cots.at[2, rows], cots.at[3, rows], cot_send.at[3 + h], cot_recv.at[3 + h], flip(1), z)
-
-    core_copy = remote(cot_ref, cots.at[1], cot_send.at[0], cot_recv.at[0], flip(1), z)
+        return remote(cots.at[2 + h, pl.ds(0, half)], cots.at[2 + h, pl.ds(half, half)], cot_send.at[4 + h], cot_recv.at[4 + h], flip(1), z)
+
+    def core_copy(h):
+        rows = pl.ds(h * half, half)
+        return remote(cot_ref.at[rows], cots.at[h, pl.ds(half, half)], cot_send.at[h], cot_recv.at[h], flip(1), z)
 
     high_rows = coords_ref.shape[0] // 4
 
@@ -215,88 +241,84 @@
 
     w_copy(0).start()
     y_copy(0).start()
-    core_copy.start()
+    for h in range(2):
+        core_copy(h).start()
     for m in range(1, 4):
         coords_copy(m).start()
-    w_copy(1).start()
-    y_copy(1).start()
+    for p in range(1, AHEAD):
+        w_copy(p).start()
     for copy in local:
         copy.wait()
 
-    def unit(t, w, q):
+    def unit(g, w, q):
         value = lax.dot_general(
-            cots[t], ws[w, pl.ds(pl.multiple_of(q * cols, cols), cols), :],
+            cots[g], ws[w, pl.ds(q * cols, cols), :],
             (((1,), (1,)), ((), ())), preferred_element_type=jnp.float32,
         )
-        rows = pl.ds(pl.multiple_of((t % 2) * tokens, tokens), tokens)
-        parts[w + 4 * (t // 2), q, rows, :] = value.astype(jnp.bfloat16)
-
-    def return_copy(w, q):
-        i = w * CHUNKS + q
-        return remote(parts.at[4 + w, q], parts.at[2 + w, q], ret_send.at[i], ret_recv.at[i], flip(4), z)
+        parts[w + 4 * (g // 2), q, g % 2] = value.astype(jnp.bfloat16)
+
+    def return_copy(w, q, h):
+        return remote(parts.at[4 + w, q, h], parts.at[2 + w, q, h], ret_send.at[w, q, h], ret_recv.at[w, q, h], flip(4), z)
 
     def owner(e):
         y = 1 - y_bit if e & 2 else y_bit
         x = 1 - x_bit if e & 1 else x_bit
         return y * 2 + x
 
-    def accumulate(e, q, slots):
-        def body(i, carry):
-            rows = pl.ds(pl.multiple_of(i * 64, 64), 64)
-            value = parts[e, q, rows, :].astype(jnp.float32)
-            for slot in slots:
-                value = value + z_got[slot, q, rows, :].astype(jnp.float32)
-            parts[e, q, rows, :] = value.astype(jnp.bfloat16)
-            return carry
-        lax.fori_loop(0, 2 * tokens // 64, body, 0)
-
-    def right_copy(e, q):
+    def accumulate(e, q, h, slot):
+        for part in (0, 1) if e < 2 else (h,):
+            def body(i, carry):
+                rows = pl.ds(pl.multiple_of(i * 64, 64), 64)
+                value = parts[e, q, part, rows, :].astype(jnp.float32) + z_got[slot, q, part, rows, :].astype(jnp.float32)
+                parts[e, q, part, rows, :] = value.astype(jnp.bfloat16)
+                return carry
+            lax.fori_loop(0, 2 * half // 64, body, 0)
+
+    def right_copy(e, q, h):
         s = owner(e)
-        return remote(parts.at[e, q], z_got.at[s + 1, q], z_send.at[e, q], z_recv.at[s + 1, q], me, lax.rem(z + 1, z_n))
-
-    def left_copy(e, q):
+        src, dst = (parts.at[e, q], z_got.at[s + 1, q]) if e < 2 else (parts.at[e, q, h], z_got.at[s + 1, q, h])
+        return remote(src, dst, z_send.at[e, q, h], z_recv.at[s + 1, q, h], me, lax.rem(z + 1, z_n))
+
+    def left_copy(e, q, h):
         s = owner(e)
-        return remote(parts.at[e, q], z_got.at[s, q], z_send.at[e, q], z_recv.at[s, q], me, lax.rem(z + z_n - 1, z_n))
-
-    def z_round(e, q, k):
+        src, dst = (parts.at[e, q], z_got.at[s, q]) if e < 2 else (parts.at[e, q, h], z_got.at[s, q, h])
+        return remote(src, dst, z_send.at[e, q, h], z_recv.at[s, q, h], me, lax.rem(z + z_n - 1, z_n))
+
+    def z_round(e, q, h, k):
         s = owner(e)
         if k < z_n:
             @pl.when((z == k - 1) & (z < s))
             def _():
                 if k > 1:
-                    right_copy(e, q).wait_recv()
-                    accumulate(e, q, [s + 1])
-                right_copy(e, q).start()
+                    right_copy(e, q, h).wait_recv()
+                    accumulate(e, q, h, s + 1)
+                right_copy(e, q, h).start()
 
             @pl.when((z == z_n - k) & (z > s))
             def _():
                 if k > 1:
-                    left_copy(e, q).wait_recv()
-                    accumulate(e, q, [s])
-                left_copy(e, q).start()
+                    left_copy(e, q, h).wait_recv()
+                    accumulate(e, q, h, s)
+                left_copy(e, q, h).start()
         else:
             @pl.when(z == s)
             def _():
                 @pl.when(z > 0)
                 def _():
-                    right_copy(e, q).wait_recv()
-                    accumulate(e, q, [s + 1])
+                    right_copy(e, q, h).wait_recv()
+                    accumulate(e, q, h, s + 1)
 
                 @pl.when(z < z_n - 1)
                 def _():
-                    left_copy(e, q).wait_recv()
-                    accumulate(e, q, [s])
-                fin_copy(e, q).start()
-                grad_ref[:, pl.ds(pl.multiple_of((core * CHUNKS + q) * cols, cols), cols)] = parts[e, q, :tokens, :]
-
-    def fin_copy(e, q):
-        return remote(parts.at[e, q, pl.ds(tokens, tokens)], fin_got.at[q], fin_send.at[q], fin_recv.at[q], flip(1), z)
-
-    def two_units(base, w, q):
-        def body(t, carry):
-            unit(base + t, w, q)
-            return carry
-        lax.fori_loop(0, 2, body, 0)
+                    left_copy(e, q, h).wait_recv()
+                    accumulate(e, q, h, s)
+                at = pl.ds(pl.multiple_of((core * CHUNKS + q) * cols, cols), cols)
+                for part in (0, 1) if e < 2 else (h,):
+                    fin_copy(e, q, part).start()
+                    grad_ref[pl.ds(part * half, half), at] = parts[e, q, part, :half, :]
+
+    def fin_copy(e, q, h):
+        return remote(parts.at[e, q, h, pl.ds(half, half)], fin_got.at[q, h], fin_send.at[q, h], fin_recv.at[q, h], flip(1), z)
 
     def project():
         b = y_bit * 2 + core
@@ -304,9 +326,13 @@
         width = cols
         def body(i, carry):
             at = pl.ds(pl.multiple_of(i * width, width), width)
-            value = jnp.dot(coords_ref[own, :], cots[0, :, at], preferred_element_type=jnp.float32)
-            for m in range(1, 4):
-                value = value + jnp.dot(coords_got[m - 1], cots[m, :, at], preferred_element_type=jnp.float32)
+            value = 0.0
+            for g in range(4):
+                lanes = slice(g % 2 * half, (g % 2 + 1) * half)
+                pair = (coords_ref[own, lanes], coords_got[0, :, lanes]) if g < 2 else (coords_got[1, :, lanes], coords_got[2, :, lanes])
+                value = value + jnp.dot(
+                    jnp.concatenate(pair, axis=1), cots[g, :, at], preferred_element_type=jnp.float32
+                )
             proj[:, at] = value
             return carry
         lax.fori_loop(0, proj.shape[1] // width, body, 0)
@@ -363,68 +389,69 @@
             dir_copy(m).wait()
         dirs_out_ref[...] = dirs[...].reshape(dirs_out_ref.shape)
 
-    def before(i):
-        e, q = ORDER[i]
-        if i == 0:
-            def body(j, carry):
-                unit(0, 0, j)
-                return carry
-            lax.fori_loop(0, CHUNKS, body, 0)
-            core_copy.wait()
-        if e == 0:
-            unit(1, 0, q)
-        if e == 1:
-            w_copy(q).wait()
-            if q + 2 < CHUNKS:
-                w_copy(q + 2).start()
-            two_units(0, 1, q)
-        if e >= 2:
-            return_copy(e - 2, q).wait()
-
-    def after(i):
-        e, q = ORDER[i]
-        if (e, q) == (1, 0):
-            y_copy(0).wait()
-            forward_copy(0).start()
-        if (e, q) == (1, 1):
-            y_copy(1).wait()
-            forward_copy(1).start()
+    def take_weight(q):
+        w_copy(q).wait()
+        if q + AHEAD < CHUNKS:
+            w_copy(q + AHEAD).start()
+        for g in range(2):
+            unit(g, 1, q)
+
+    def own_units(q):
+        if q == 0:
             for h in range(2):
-                forward_copy(h).wait_recv()
-            for w, p in ((0, 0), (0, 1), (0, 2), (0, 3), (1, 0), (1, 1)):
-                two_units(2, w, p)
-                return_copy(w, p).start()
-                if (w, p) == (0, 0):
-                    for m in range(1, 4):
-                        coords_copy(m).wait()
-                    send_projected()
-        if e == 1 and q >= 2:
-            two_units(2, 1, q)
-            return_copy(1, q).start()
-
-    stages = {8: send_sums, 10: send_zsums, 12: send_dirs}
-    count = len(ORDER)
-    for i in range(count + LAG * (z_n - 1)):
-        if i < count:
-            before(i)
-            z_round(*ORDER[i], 1)
-            after(i)
-        for k in range(2, z_n + 1):
-            j = i - LAG * (k - 1)
-            if 0 <= j < count:
-                z_round(*ORDER[j], k)
-        if i in stages:
-            stages[i]()
+                core_copy(h).wait()
+        for g in range(2):
+            unit(g, 0, q)
+
+    taken = []
+
+    def forwarded(h):
+        if h not in taken:
+            forward_copy(h).wait_recv()
+            taken.append(h)
+
+    for kind, *at in ORDER:
+        if kind == START:
+            y_copy(1).start()
+        elif kind == OWN:
+            own_units(*at)
+        elif kind == X:
+            take_weight(*at)
+        elif kind == Y:
+            y_copy(*at).wait()
+            forward_copy(*at).start()
+        elif kind == BACK:
+            e, q, h = at
+            forwarded(h)
+            unit(2 + h, e - 2, q)
+            return_copy(e - 2, q, h).start()
+        elif kind == Z:
+            e, q, h, k = at
+            if e >= 2 and k == 1:
+                return_copy(e - 2, q, h).wait()
+            z_round(e, q, h, k)
+        elif kind == PROJECT:
+            for h in range(2):
+                forwarded(h)
+            for m in range(1, 4):
+                coords_copy(m).wait()
+            send_projected()
+        else:
+            {SUMS: send_sums, ZSUMS: send_zsums, DIRS: send_dirs}[kind]()
     take_dirs()
     for q in range(CHUNKS):
-        fin_copy(0, q).wait()
-        grad_ref[:, pl.ds(pl.multiple_of(((1 - core) * CHUNKS + q) * cols, cols), cols)] = fin_got[q]
+        for h in range(2):
+            fin_copy(0, q, h).wait()
+            at = pl.ds(pl.multiple_of(((1 - core) * CHUNKS + q) * cols, cols), cols)
+            grad_ref[pl.ds(h * half, half), at] = fin_got[q, h]
     for h in range(2):
         forward_copy(h).wait_send()
-    for e, q in ORDER:
+    for e in range(4):
         @pl.when(z != owner(e))
         def _():
-            right_copy(e, q).wait_send()
+            for q in range(CHUNKS):
+                for h in range(1 if e < 2 else 2):
+                    right_copy(e, q, h).wait_send()
 
 
 def exchange(z_n, cotangent, gate_weight, coords, first_moment, second_moment):
@@ -451,9 +478,9 @@
         scratch_shapes=[
             pltpu.VMEM((4, tokens, hidden), bf16),
             pltpu.VMEM((2, w_rows, hidden), bf16),
-            pltpu.VMEM((6, CHUNKS, 2 * tokens, cols), bf16),
-            pltpu.VMEM((z_n + 1, CHUNKS, 2 * tokens, cols), bf16),
-            pltpu.VMEM((CHUNKS, tokens, cols), bf16),
+            pltpu.VMEM((6, CHUNKS, 2, tokens, cols), bf16),
+            pltpu.VMEM((z_n + 1, CHUNKS, 2, tokens, cols), bf16),
+            pltpu.VMEM((CHUNKS, 2, tokens // 2, cols), bf16),
             pltpu.VMEM((3, rank // 4, tokens), bf16),
             pltpu.VMEM((2 * own, hidden), f32),
             pltpu.VMEM((own, hidden), bf16),
@@ -461,12 +488,12 @@
             pltpu.VMEM((8, 8, 128), f32),
             pltpu.VMEM((z_n, 8, 128), f32),
             pltpu.VMEM((8, own, hidden), bf16),
-            dma((2,)),
-            dma((5,)), dma((5,)),
+            dma((3,)),
+            dma((6,)), dma((6,)),
             dma((CHUNKS,)), dma((CHUNKS,)),
-            dma((2 * CHUNKS,)), dma((2 * CHUNKS,)),
-            dma((4, CHUNKS)), dma((z_n + 1, CHUNKS)),
-            dma((CHUNKS,)), dma((CHUNKS,)),
+            dma((2, CHUNKS, 2)), dma((2, CHUNKS, 2)),
+            dma((4, CHUNKS, 2)), dma((z_n + 1, CHUNKS, 2)),
+            dma((CHUNKS, 2)), dma((CHUNKS, 2)),
             dma((3,)), dma((3,)),
             dma, dma,
             dma((8,)), dma((8,)),

time: 299 us -> 253 us (0.85)
  Pallas kernels: 281 us -> 234 us
    pallas_call x1, Pallas kernels: 281 us -> 234 us  [exchange(): pl.pallas_call(functools.partial(exchange_kernel, z_n), out_shape=[jax.Sh...]
where the time goes in v3:
time: 253 us
  Pallas kernels  234 us (92%)
  matrix products  14 us (6%)
  local copies, waits for them, and re-layouts  3.59 us (1%)
    pallas_call x1, Pallas kernels, exchange(): pl.pallas_call(functools.partial(exchange_kernel, z_n), out_shape=[jax.Sh...  234 us
    dot_general x1, matrix products, on_pairs(): lax.dot_general(basis, activations, (((0,), (1,)), ((), ())), preferred_e...  7.04 us
    dot_general x1, matrix products, on_pairs(): jnp.dot(basis_rows, direction, preferred_element_type=jnp.float32)  6.93 us

profile of v3, /device:TPU:7, one launch (start us, length us, event | category | flops | bytes accessed | tf_op | source)
XLA Modules:
  0.0 252.6 jit_solution(1027988780349427620)
XLA Ops:
  0.6 7.0 %convolution_convert_fusion.1 = bf16[256,512]{1,0:T(8,128)(2,1)S(1)} fusion(bf16[8192,256]{1,0:T(8,128)(2,1)} %param.9, bf16[512,8192]{1,0:T(8,128)(2,1)} %param.6), kind=kOutput, calls=%fused_computation.1 | convolution fusion | flops 2147614720 | bytes 12845056 | tf_op jit(solution)/shard_map/dot_general | solution.py:515
  7.7 0.7 copy.10
  8.4 234.3 %shard_map.93 = (bf16[512,2048]{1,0:T(8,128)(2,1)}, f32[32,3584]{1,0:T(8,128)}, f32[32,3584]{1,0:T(8,128)}, bf16[256,3584]{1,0:T(8,128)(2,1)}) custom-call(bf16[512,3584]{1,0:T(8,128)(2,1)} %cot_ref.1, bf16[1024,3584]{1,0:T(8,128)(2,1)} %w_ref.1, bf16[256,512]{1,0:T(8,128)(2,1)} %bitcast.7, f32[32,3584]{1,0:T(8,128)} %first_ref.1, f32[32,3584]{1,0:T(8,128)} %second_ref.1), custom_call_target="tpu_custom_call" | custom-call | flops 30064771072 | bytes 24000000 | tf_op jit(solution)/shard_map/pallas_call | solution.py:468
  242.8 0.0 copy-start
  242.8 6.9 %convolution_convert_fusion = bf16[1024,3584]{1,0:T(8,128)(2,1)} fusion(bf16[256,3584]{1,0:T(8,128)(2,1)} %get-tuple-element.9, bf16[8192,256]{1,0:T(8,128)(2,1)} %param.9, s32[]{:T(128)S(6)} %select_n.3), kind=kOutput, calls=%fused_computation | convolution fusion | flops 1882718208 | bytes 9699332 | tf_op jit(solution)/shard_map/dot_general | solution.py:523
  249.7 0.0 copy-done
  249.7 0.0 copy-start.2
  249.7 0.0 copy-start.1
  249.7 1.3 copy.14
  251.0 0.0 copy-done.2
  251.0 0.8 copy.15
  251.8 0.0 copy-done.1
  251.8 0.8 copy.16
Async XLA Ops:
  242.8 6.9 %copy-start = (bf16[512,2048]{1,0:T(8,128)(2,1)S(1)}, bf16[512,2048]{1,0:T(8,128)(2,1)}, u32[]{:S(2)}) copy-start(bf16[512,2048]{1,0:T(8,128)(2,1)} %get-tuple-element.16) | copy-start | bytes 6291460
  249.7 1.3 copy-start.2
  249.7 2.1 copy-start.1
